TPU v7x, 256 devices: a whole 4x4x8 slice. The times are simulated.
256 devices in a mesh: dom: 128 (over y, x, z), col: 2 (over core).
Axes of the slice: x: 4, y: 4, z: 8, core: 2. Of those that a mesh axis runs over, the one named last changes fastest.
Arguments:
- features: bfloat16 [131072, 256], P(('dom', 'col')), may hold values from -6 to 6
- weight: bfloat16 [256, 256], replicated, may hold values from -0.375 to 0.375
- cotangent: bfloat16 [131072, 256], P(('dom', 'col')), may hold values from -6 to 6
- tile_values: bfloat16 [10240, 128, 128], P(('dom', 'col')), may hold values from -0.15625 to 0.15625
- tile_rows: int32 [10240], P(('dom', 'col')), may hold values from 0 to 7
- tile_cols: int32 [10240], P(('dom', 'col')), may hold values from 0 to 131, as said below
- tile_count: int32 [256], P(('dom', 'col')), may hold values from 20 to 40, as said below
- send_blocks: int32 [256, 128], P(('dom', 'col')), may hold values from 0 to 3
Outputs:
- output_rows: bfloat16 [131072, 256], P(('dom', 'col'))
- feature_grad: bfloat16 [131072, 256], P(('dom', 'col'))
- weight_grad: float32 [256, 256], replicated
Inputs may be any that keep to these rules, and one draw needn't show every extreme that they name: `tile_cols`: A value v below 4 names the device's own row block v; a value 4 + s names the row block that the device of partition s with the same col index sends to this partition; no receive slot is named by two tiles of one device. Only the first tile_count slots of a device's tiles are live; some device has all 40 live.
All inputs are finite; a program needn't handle non-finite values.
Results may differ from a plain program's by a relative error of at most 0.0049.
Values may be sent and summed in bfloat16 or wider, within the bound.
No kernel may reach another device: no remote copies, remote signals or barrier semaphores. Data moves between devices by JAX's collectives and lax.ppermute only.
A program may use at most 128 MiB of HBM per device.

v0:
```python
import jax
import jax.numpy as jnp
from jax import lax
from jax.sharding import PartitionSpec as P


def in_one_piece(arrays, axis, split_dim, concat_dim, along):
    ends, at = ([], 0)
    for a in arrays[:-1]:
        at += a.shape[along]
        ends.append(at)
    both = jnp.concatenate(arrays, axis=along)
    return tuple(
        jnp.split(
            lax.all_to_all(both, axis, split_axis=split_dim, concat_axis=concat_dim, tiled=True),
            ends,
            axis=along,
        )
    )


def local(features, weight, cotangent, tile_values, tile_rows, tile_cols, tile_count, send_blocks):
    block_size = tile_values.shape[1]
    half_blocks = features.shape[0] // block_size
    width_in = features.shape[1]
    peer_count = send_blocks.shape[1]
    all_blocks = half_blocks * lax.axis_size("col")
    node_total = features.shape[0] * lax.axis_size("col") * lax.axis_size("dom")
    own_blocks = features.reshape(half_blocks, block_size, width_in)
    outgoing = own_blocks[send_blocks[0]]
    incoming = lax.all_to_all(outgoing, "dom", split_axis=0, concat_axis=0, tiled=True)
    sources = jnp.concatenate([own_blocks, incoming], axis=0)
    live_bool = jnp.arange(tile_values.shape[0], dtype=jnp.int32) < tile_count[0]
    live_mask = live_bool.astype(jnp.bfloat16)
    masked_tiles = tile_values * live_mask[:, None, None]
    picked = sources[tile_cols]
    products = jnp.einsum("tij,tjf->tif", masked_tiles, picked, preferred_element_type=jnp.float32)
    partial_value = jax.ops.segment_sum(products, tile_rows, num_segments=all_blocks)
    summed = lax.psum_scatter(partial_value, "col", scatter_dimension=0, tiled=True)
    hidden = summed.astype(jnp.bfloat16).reshape(half_blocks * block_size, width_in)
    output_rows = jnp.dot(hidden, weight, preferred_element_type=jnp.float32).astype(jnp.bfloat16)
    own_grad = lax.dot_general(
        cotangent, weight, (((1,), (1,)), ((), ())), preferred_element_type=jnp.float32
    ).astype(jnp.bfloat16)
    own_grad = own_grad.reshape(half_blocks, block_size, width_in)
    grad_blocks = lax.all_gather(own_grad, "col", axis=0, tiled=True)
    chosen = grad_blocks[tile_rows]
    is_local = tile_cols < half_blocks
    local_tiles = masked_tiles * is_local.astype(jnp.bfloat16)[:, None, None]
    back_terms = jnp.einsum("tji,tjf->tif", local_tiles, chosen, preferred_element_type=jnp.float32)
    local_ids = jnp.where(is_local, tile_cols, 0)
    own_part = jax.ops.segment_sum(back_terms, local_ids, num_segments=half_blocks)
    slot_ids = half_blocks + jnp.arange(peer_count, dtype=jnp.int32)
    matches = ((tile_cols[:, None] == slot_ids[None, :]) & live_bool[:, None]).astype(jnp.bfloat16)
    slot_tiles = jnp.einsum(
        "ts,tij->sij", matches, tile_values, preferred_element_type=jnp.float32
    ).astype(jnp.bfloat16)
    slot_grads = jnp.einsum(
        "ts,tjf->sjf", matches, chosen, preferred_element_type=jnp.float32
    ).astype(jnp.bfloat16)
    back_tiles, back_grads = in_one_piece((slot_tiles, slot_grads), "dom", 0, 0, 2)
    remote_terms = jnp.einsum(
        "sji,sjf->sif", back_tiles, back_grads, preferred_element_type=jnp.float32
    )
    grad_total = own_part + jax.ops.segment_sum(
        remote_terms, send_blocks[0], num_segments=half_blocks
    )
    feature_grad = grad_total.astype(jnp.bfloat16).reshape(half_blocks * block_size, width_in)
    local_weight = lax.dot_general(
        hidden, cotangent, (((0,), (0,)), ((), ())), preferred_element_type=jnp.float32
    )
    local_weight = local_weight * jnp.float32(1.0 / node_total**0.5)
    weight_grad = lax.psum(local_weight, ("dom", "col"))
    return (output_rows, feature_grad, weight_grad)


def solution(mesh):
    return jax.shard_map(
        local,
        mesh=mesh,
        in_specs=(
            P(("dom", "col"), None),
            P(),
            P(("dom", "col"), None),
            P(("dom", "col"), None, None),
            P(("dom", "col")),
            P(("dom", "col")),
            P(("dom", "col")),
            P(("dom", "col"), None),
        ),
        out_specs=(P(("dom", "col"), None), P(("dom", "col"), None), P()),
        check_vma=False,
    )
```

profile of v0, /device:TPU:2, one launch (start us, length us, event | category | flops | bytes accessed | tf_op | source)
XLA Modules:
  0.0 573.9 jit_solution(5552977802668099284)
XLA Ops:
  7.2 0.0 copy-start
  7.2 0.7 fusion.21
  7.9 7.5 %gather_fusion = bf16[128,128,256]{2,1,0:T(8,128)(2,1)} fusion(bf16[4,128,256]{2,1,0:T(8,128)(2,1)} %bitcast.25, s32[1024]{0:T(1024)S(1)} %pad_clamp_fusion.2), kind=kCustom, calls=%fused_computation | custom fusion | bytes 16777728 | tf_op jit(solution)/shard_map/gather | solution.py:30
  15.4 16.0 %all-to-all-start = ((bf16[128,128,256]{2,1,0:T(8,128)(2,1)}), bf16[128,128,256]{2,1,0:T(8,128)(2,1)}, u32[]{:S(2)}, u32[]{:S(2)}) async-start(bf16[128,128,256]{2,1,0:T(8,128)(2,1)} %gather_fusion), calls=%async_computation | async-start | bytes 16777216 | tf_op jit(solution)/shard_map/all_to_all | solution.py:31
  32.0 0.0 copy-done.5
  32.0 0.0 copy-done.8
  32.0 3.8 convolution_convert_fusion.1
  35.8 6.4 %copy.26 = bf16[128,128,128]{2,0,1:T(8,128)(2,1)} copy(bf16[128,128,128]{0,2,1:T(8,128)(2,1)} %convolution_convert_fusion.1) | data formatting | bytes 8388608 | tf_op jit(solution)/shard_map/convert_element_type | solution.py:57
  42.2 0.0 copy-done.9
  42.2 0.0 copy-done
  42.2 0.0 copy-done.7
  42.3 0.3 convolution_convert_fusion.2
  42.5 2.4 all_gather.3
  44.9 0.7 gather_fusion.2
  45.6 0.0 copy-start.3
  45.6 0.0 copy-start.4
  45.6 2.5 convolution_convert_fusion
  48.1 0.0 copy-done.3
  48.1 0.7 copy-done.4
  48.7 2.3 pad_maximum_fusion
  51.0 29.1 %copy.27 = bf16[128,128,384]{2,1,0:T(8,128)(2,1)} copy(bf16[128,128,384]{2,0,1:T(8,128)(2,1)S(1)} %pad_maximum_fusion) | data formatting | bytes 25165824 | tf_op jit(solution)/shard_map/concatenate | solution.py:12
  80.1 136.3 %all-to-all-done = bf16[128,128,256]{2,1,0:T(8,128)(2,1)} async-done(((bf16[128,128,256]{2,1,0:T(8,128)(2,1)}), bf16[128,128,256]{2,1,0:T(8,128)(2,1)}, u32[]{:S(2)}, u32[]{:S(2)}) %all-to-all-start) | async-done | bytes 8388640 | tf_op jit(solution)/shard_map/all_to_all | solution.py:31
  216.4 11.2 %all-to-all-start.1 = ((bf16[128,128,384]{2,1,0:T(8,128)(2,1)}), bf16[128,128,384]{2,1,0:T(8,128)(2,1)}, u32[]{:S(2)}, u32[]{:S(2)}) async-start(bf16[128,128,384]{2,1,0:T(8,128)(2,1)} %copy.27), calls=%async_computation.2 | async-start | bytes 25165824 | tf_op jit(solution)/shard_map/all_to_all | solution.py:15
  227.6 0.3 reduce-scatter.2.cloned.1.call-start
  227.9 0.0 copy-done.1
  227.9 7.5 %pad_maximum_fusion.1 = bf16[132,128,256]{2,1,0:T(8,128)(2,1)} fusion(bf16[128,128,256]{2,1,0:T(8,128)(2,1)} %all-to-all-done, bf16[4,128,256]{2,1,0:T(8,128)(2,1)S(1)} %bitcast.26), kind=kLoop, calls=%fused_computation.7 | loop fusion | flops 4325376 | bytes 17301504 | tf_op jit(solution)/shard_map/concatenate | solution.py:32
  235.4 6.0 %gather_fusion.1 = bf16[40,128,256]{2,1,0:T(8,128)(2,1)} fusion(bf16[132,128,256]{2,1,0:T(8,128)(2,1)} %pad_maximum_fusion.1, s32[1024]{0:T(1024)S(1)} %pad_clamp_fusion.1), kind=kCustom, calls=%fused_computation.1 | custom fusion | bytes 5243040 | tf_op jit(solution)/shard_map/gather | solution.py:36
  241.5 0.0 copy-done.6
  241.5 4.9 fusion.8
  246.4 0.1 broadcast_in_dim.12
  246.5 0.0 copy-done.10
  246.5 9.0 %scatter_fusion = f32[8,128,256]{2,1,0:T(8,128)S(1)} fusion(f32[8,128,256]{2,1,0:T(8,128)S(1)} %broadcast_in_dim.12, s32[40]{0:T(128)S(1)} %copy-done.10, f32[40,128,256]{2,1,0:T(8,128)} %fusion.8), kind=kCustom, calls=%fused_computation.3 | custom fusion | flops 1310720 | bytes 15728800 | tf_op jit(solution)/shard_map/scatter-add | solution.py:38
  255.6 1.0 copy-done.2
  256.5 0.0 reduce-scatter.2.cloned.1.call-update
  256.6 0.0 all-reduce.2.cloned.1.call-start
  256.6 5.3 fusion.5
  261.9 9.1 %scatter_fusion.1 = f32[4,128,256]{2,1,0:T(8,128)S(1)} fusion(f32[4,128,256]{2,1,0:T(8,128)S(1)} %broadcast.41.clone, s32[40]{0:T(128)S(1)} %get-tuple-element.3, f32[40,128,256]{2,1,0:T(8,128)} %fusion.5), kind=kCustom, calls=%fused_computation.4 | custom fusion | flops 1310720 | bytes 15728800 | tf_op jit(solution)/shard_map/scatter-add | solution.py:52
  271.1 0.9 reduce-scatter.2.cloned.1.call-done
  272.0 1.1 convert_element_type.30
  273.0 1.0 convolution_multiply_fusion
  274.0 0.0 all-reduce.2.cloned.1.call-update
  274.0 0.9 convolution_convert_fusion.3
  275.0 227.1 %all-to-all-done.1 = bf16[128,128,384]{2,1,0:T(8,128)(2,1)} async-done(((bf16[128,128,384]{2,1,0:T(8,128)(2,1)}), bf16[128,128,384]{2,1,0:T(8,128)(2,1)}, u32[]{:S(2)}, u32[]{:S(2)}) %all-to-all-start.1) | async-done | bytes 12582944 | tf_op jit(solution)/shard_map/all_to_all | solution.py:15
  502.1 12.8 %fusion = f32[128,128,256]{2,1,0:T(8,128)} fusion(bf16[128,128,384]{2,1,0:T(8,128)(2,1)} %all-to-all-done.1), kind=kOutput, calls=%fused_computation.8 | convolution fusion | flops 1073741824 | bytes 29360128 | tf_op jit(solution)/shard_map/sji,sjf->sif/dot_general | solution.py:62
  514.9 24.1 %scatter_fusion.2 = f32[4,128,256]{2,1,0:T(8,128)S(1)} fusion(f32[4,128,256]{2,1,0:T(8,128)S(1)} %broadcast.41.clone.1, s32[128]{0:T(128)S(1)} %bitcast.31, f32[128,128,256]{2,1,0:T(8,128)} %fusion), kind=kCustom, calls=%fused_computation.5 | custom fusion | flops 4194304 | bytes 50332160 | tf_op jit(solution)/shard_map/scatter-add | solution.py:65
  539.0 0.8 add_convert_fusion
  539.8 25.6 %all-reduce.2.cloned.1.call-done = f32[256,256]{1,0:T(8,128)} async-done(((f32[256,256]{1,0:T(8,128)}), f32[256,256]{1,0:T(8,128)}) %all-reduce.2.cloned.1.call-update) | async-done | bytes 262160 | tf_op jit(solution)/shard_map/psum | solution.py:73
  565.4 1.7 copy.40
  (21 shorter events, 0.1 us)
Async XLA Ops:
  7.2 35.1 %copy-start = (bf16[512,256]{1,0:T(8,128)(2,1)S(1)}, bf16[512,256]{1,0:T(8,128)(2,1)}, u32[]{:S(2)}) copy-start(bf16[512,256]{1,0:T(8,128)(2,1)} %param.10) | copy-start | bytes 786436
  15.3 16.7 %copy-start.5 = (bf16[40,128,128]{2,1,0:T(8,128)(2,1)S(1)}, bf16[40,128,128]{2,1,0:T(8,128)(2,1)}, u32[]{:S(2)}) copy-start(bf16[40,128,128]{2,1,0:T(8,128)(2,1)} %param.11) | copy-start | bytes 3932164
  15.3 16.7 %copy-start.8 = (s32[40]{0:T(128)S(1)}, s32[40]{0:T(128)}, u32[]{:S(2)}) copy-start(s32[40]{0:T(128)} %param.13) | copy-start | bytes 484
  15.4 201.0 %all-to-all-start = ((bf16[128,128,256]{2,1,0:T(8,128)(2,1)}), bf16[128,128,256]{2,1,0:T(8,128)(2,1)}, u32[]{:S(2)}, u32[]{:S(2)}) async-start(bf16[128,128,256]{2,1,0:T(8,128)(2,1)} %gather_fusion), calls=%async_computation | async-start | bytes 16777216 | tf_op jit(solution)/shard_map/all_to_all | solution.py:31
  35.8 6.4 %copy-start.9 = (s32[40]{0:T(128)S(1)}, s32[40]{0:T(128)}, u32[]{:S(2)}) copy-start(s32[40]{0:T(128)} %param.12) | copy-start | bytes 484
  35.8 6.4 %copy-start.7 = (bf16[256,256]{1,0:T(8,128)(2,1)S(1)}, bf16[256,256]{1,0:T(8,128)(2,1)}, u32[]{:S(2)}) copy-start(bf16[256,256]{1,0:T(8,128)(2,1)} %param.9) | copy-start | bytes 393220
  45.6 2.5 copy-start.3
  45.6 3.1 copy-start.4
  80.1 147.8 %copy-start.1 = (bf16[512,256]{1,0:T(8,128)(2,1)S(1)}, bf16[512,256]{1,0:T(8,128)(2,1)}, u32[]{:S(2)}) copy-start(bf16[512,256]{1,0:T(8,128)(2,1)} %param.8) | copy-start | bytes 786436
  216.4 285.7 %all-to-all-start.1 = ((bf16[128,128,384]{2,1,0:T(8,128)(2,1)}), bf16[128,128,384]{2,1,0:T(8,128)(2,1)}, u32[]{:S(2)}, u32[]{:S(2)}) async-start(bf16[128,128,384]{2,1,0:T(8,128)(2,1)} %copy.27), calls=%async_computation.2 | async-start | bytes 25165824 | tf_op jit(solution)/shard_map/all_to_all | solution.py:15
  227.6 44.4 %reduce-scatter.2.cloned.1.call-start = ((), (), s32[]{:S(2)}) async-start(), calls=%async_computation.3 | async-start | bytes 1572864 | tf_op jit(solution)/shard_map/reduce_scatter | solution.py:39
  235.4 6.0 %copy-start.6 = (bf16[40,128,128]{2,1,0:T(8,128)(2,1)S(1)}, bf16[40,128,128]{2,1,0:T(8,128)(2,1)}, u32[]{:S(2)}) copy-start(bf16[40,128,128]{2,1,0:T(8,128)(2,1)} %param.11) | copy-start | bytes 3932164
  241.5 5.0 copy-start.10
  255.6 1.0 copy-start.2
  256.6 308.9 %all-reduce.2.cloned.1.call-start = ((), (), s32[]{:S(2)}) async-start(), calls=%async_computation.4 | async-start | bytes 524288 | tf_op jit(solution)/shard_map/psum | solution.py:73
  275.0 239.9 %copy-start.11 = (s32[1,128]{1,0:T(1,128)S(1)}, s32[1,128]{1,0:T(1,128)}, u32[]{:S(2)}) copy-start(s32[1,128]{1,0:T(1,128)} %param.15) | copy-start | bytes 1540
Sparse Core Ops, SparseCore 0:
  256.7 15.2 reduce-scatter.1
  278.9 286.4 all-reduce.1
where the time goes:
time: 575 us; the launch traced here: 574 us
  waiting for transfers between devices  390 us (68%)
  other arithmetic  54.6 us (9%)
  local copies, waits for them, and re-layouts  53.2 us (9%)
  matrix products  31.4 us (5%)
  starting transfers between devices  27.5 us (5%)
  between operations  14.9 us (3%)
    all_to_all x1, waiting for transfers between devices, in_one_piece(): lax.all_to_all(both, axis, split_axis=split_dim, concat_axis=concat_dim,...  227 us
    all_to_all x1, waiting for transfers between devices, local(): lax.all_to_all(outgoing, 'dom', split_axis=0, concat_axis=0, tiled=True)  136 us
    concatenate x1, local copies, waits for them, and re-layouts, in_one_piece(): both = jnp.concatenate(arrays, axis=along)  29.1 us
    psum x1, waiting for transfers between devices, local(): weight_grad = lax.psum(local_weight, ('dom', 'col'))  25.6 us
    scatter-add x1, other arithmetic, local(): jax.ops.segment_sum(remote_terms, send_blocks[0], num_segments=half_blocks)  24.1 us
    all_to_all x1, starting transfers between devices, local(): lax.all_to_all(outgoing, 'dom', split_axis=0, concat_axis=0, tiled=True)  16 us
    dot_general x1, matrix products, local(): jnp.einsum('sji,sjf->sif', back_tiles, back_grads, preferred_element_type...  12.8 us
  transfers between devices with their start and end apart: 4, of which 4 were waited for; matrix products, arithmetic and copies ran while one was open for 22% of the time, Pallas kernels for 0%

commit v1 on v0

--- a/solution.py
+++ b/solution.py
@@ -70,7 +70,7 @@
         hidden, cotangent, (((0,), (0,)), ((), ())), preferred_element_type=jnp.float32
     )
     local_weight = local_weight * jnp.float32(1.0 / node_total**0.5)
-    weight_grad = lax.psum(local_weight, ("dom", "col"))
+    weight_grad = jnp.sum(lax.all_gather(local_weight, ("dom", "col")), axis=0)
     return (output_rows, feature_grad, weight_grad)
 
 

time: 575 us -> 782 us (1.36)
  waiting for transfers between devices: 390 us -> 570 us
  other arithmetic: 54.6 us -> 76.7 us
    all_to_all x1, waiting for transfers between devices: 227 us -> 377 us  [in_one_piece(): lax.all_to_all(both, axis, split_axis=split_dim, concat_axis=concat_dim,...]
    all_to_all x1, waiting for transfers between devices: 136 us -> 184 us  [local(): lax.all_to_all(outgoing, 'dom', split_axis=0, concat_axis=0, tiled=True)]
    psum x1 -> x0, waiting for transfers between devices: 25.6 us -> none  [local(): weight_grad = lax.psum(local_weight, ('dom', 'col'))]
    reduce_sum x0 -> x1, other arithmetic: none -> 21.8 us  [local(): weight_grad = jnp.sum(lax.all_gather(local_weight, ('dom', 'col')), axis=0)]
    reduce_scatter x1, waiting for transfers between devices: 0.91 us -> 9.87 us  [local(): lax.psum_scatter(partial_value, 'col', scatter_dimension=0, tiled=True)]
  transfers between devices with their start and end apart: 4 -> 4, of which waited for: 4 -> 3; matrix products, arithmetic and copies ran while one was open for 22% -> 13% of each run, Pallas kernels for 0% -> 0%
where the time goes in v1:
time: 782 us; the launch traced here: 778 us
  waiting for transfers between devices  570 us (73%)
  other arithmetic  76.7 us (10%)
  local copies, waits for them, and re-layouts  51.5 us (7%)
  matrix products  32.2 us (4%)
  starting transfers between devices  30.2 us (4%)
  between operations  14.9 us (2%)
    all_to_all x1, waiting for transfers between devices, in_one_piece(): lax.all_to_all(both, axis, split_axis=split_dim, concat_axis=concat_dim,...  377 us
    all_to_all x1, waiting for transfers between devices, local(): lax.all_to_all(outgoing, 'dom', split_axis=0, concat_axis=0, tiled=True)  184 us
    concatenate x1, local copies, waits for them, and re-layouts, in_one_piece(): both = jnp.concatenate(arrays, axis=along)  29 us
    scatter-add x1, other arithmetic, local(): jax.ops.segment_sum(remote_terms, send_blocks[0], num_segments=half_blocks)  24.1 us
    reduce_sum x1, other arithmetic, local(): weight_grad = jnp.sum(lax.all_gather(local_weight, ('dom', 'col')), axis=0)  21.8 us
    all_to_all x1, starting transfers between devices, local(): lax.all_to_all(outgoing, 'dom', split_axis=0, concat_axis=0, tiled=True)  16 us
  transfers between devices with their start and end apart: 4, of which 3 were waited for; matrix products, arithmetic and copies ran while one was open for 13% of the time, Pallas kernels for 0%

profile of v1, /device:TPU:2, one launch (start us, length us, event | category | flops | bytes accessed | tf_op | source)
XLA Modules:
  0.0 778.1 jit_solution(4187768351390402524)
XLA Ops:
  7.2 0.0 copy-start
  7.2 0.7 fusion.21
  7.9 7.4 gather_fusion
  15.3 16.0 %all-to-all-start = ((bf16[128,128,256]{2,1,0:T(8,128)(2,1)}), bf16[128,128,256]{2,1,0:T(8,128)(2,1)}, u32[]{:S(2)}, u32[]{:S(2)}) async-start(bf16[128,128,256]{2,1,0:T(8,128)(2,1)} %gather_fusion), calls=%async_computation | async-start | bytes 16777216 | tf_op jit(solution)/shard_map/all_to_all | solution.py:31
  31.3 0.0 reduce-scatter.2.cloned.1.call-start
  32.0 0.0 copy-done.9
  32.0 0.5 compare_select_fusion.3
  32.6 183.8 %all-to-all-done = bf16[128,128,256]{2,1,0:T(8,128)(2,1)} async-done(((bf16[128,128,256]{2,1,0:T(8,128)(2,1)}), bf16[128,128,256]{2,1,0:T(8,128)(2,1)}, u32[]{:S(2)}, u32[]{:S(2)}) %all-to-all-start) | async-done | bytes 8388640 | tf_op jit(solution)/shard_map/all_to_all | solution.py:31
  216.4 0.0 copy-done.2
  216.4 7.5 pad_maximum_fusion.1
  223.9 6.0 gather_fusion.1
  229.9 0.0 copy-done.5
  229.9 4.9 fusion.8
  234.8 0.1 broadcast_in_dim.12
  234.9 0.0 copy-done.12
  234.9 9.0 %scatter_fusion = f32[8,128,256]{2,1,0:T(8,128)S(1)} fusion(f32[8,128,256]{2,1,0:T(8,128)S(1)} %broadcast_in_dim.12, s32[40]{0:T(128)S(1)} %copy-done.12, f32[40,128,256]{2,1,0:T(8,128)} %fusion.8), kind=kCustom, calls=%fused_computation.3 | custom fusion | flops 1310720 | bytes 15728800 | tf_op jit(solution)/shard_map/scatter-add | solution.py:38
  244.0 1.0 copy-done.3
  244.9 0.0 reduce-scatter.2.cloned.1.call-update
  244.9 0.0 all-gather.3.cloned.1.call-start
  245.0 9.9 %reduce-scatter.2.cloned.1.call-done = f32[4,128,256]{2,1,0:T(8,128)} async-done(((f32[8,128,256]{2,1,0:T(8,128)}), f32[4,128,256]{2,1,0:T(8,128)}) %reduce-scatter.2.cloned.1.call-update) | async-done | bytes 524304 | tf_op jit(solution)/shard_map/reduce_scatter | solution.py:39
  254.9 1.1 convert_element_type.30
  255.9 0.0 copy-start.6
  255.9 0.7 copy-done.6
  256.6 1.0 convolution_multiply_fusion
  257.6 0.0 all-gather.3.cloned.1.call-update
  257.7 0.0 copy-start.10
  257.7 3.8 convolution_convert_fusion.1
  261.5 6.5 copy.26
  268.0 0.3 convolution_convert_fusion.2
  268.2 0.0 copy-start.11
  268.3 2.4 all_gather.9
  270.6 0.7 gather_fusion.2
  271.4 2.5 convolution_convert_fusion
  273.8 2.3 pad_maximum_fusion
  276.1 29.0 %copy.27 = bf16[128,128,384]{2,1,0:T(8,128)(2,1)} copy(bf16[128,128,384]{2,0,1:T(8,128)(2,1)S(1)} %pad_maximum_fusion) | data formatting | bytes 25165824 | tf_op jit(solution)/shard_map/concatenate | solution.py:12
  305.1 14.2 %all-to-all-start.1 = ((bf16[128,128,384]{2,1,0:T(8,128)(2,1)}), bf16[128,128,384]{2,1,0:T(8,128)(2,1)}, u32[]{:S(2)}, u32[]{:S(2)}) async-start(bf16[128,128,384]{2,1,0:T(8,128)(2,1)} %copy.27), calls=%async_computation.2 | async-start | bytes 25165824 | tf_op jit(solution)/shard_map/all_to_all | solution.py:15
  319.3 0.0 copy-start.13
  319.3 5.1 fusion.5
  324.4 0.0 copy-start.7
  324.4 9.0 %scatter_fusion.1 = f32[4,128,256]{2,1,0:T(8,128)S(1)} fusion(f32[4,128,256]{2,1,0:T(8,128)S(1)} %broadcast.41.clone, s32[40]{0:T(128)S(1)} %copy-done.13, f32[40,128,256]{2,1,0:T(8,128)} %fusion.5), kind=kCustom, calls=%fused_computation.4 | custom fusion | flops 1310720 | bytes 15728800 | tf_op jit(solution)/shard_map/scatter-add | solution.py:52
  333.5 0.0 copy-done.7
  333.5 0.9 convolution_convert_fusion.3
  334.4 376.5 %all-to-all-done.1 = bf16[128,128,384]{2,1,0:T(8,128)(2,1)} async-done(((bf16[128,128,384]{2,1,0:T(8,128)(2,1)}), bf16[128,128,384]{2,1,0:T(8,128)(2,1)}, u32[]{:S(2)}, u32[]{:S(2)}) %all-to-all-start.1) | async-done | bytes 12582944 | tf_op jit(solution)/shard_map/all_to_all | solution.py:15
  710.9 13.7 %fusion = f32[128,128,256]{2,1,0:T(8,128)} fusion(bf16[128,128,384]{2,1,0:T(8,128)(2,1)} %all-to-all-done.1), kind=kOutput, calls=%fused_computation.8 | convolution fusion | flops 1073741824 | bytes 29360128 | tf_op jit(solution)/shard_map/sji,sjf->sif/dot_general | solution.py:62
  724.7 0.0 copy-done.14
  724.7 24.1 %scatter_fusion.2 = f32[4,128,256]{2,1,0:T(8,128)S(1)} fusion(f32[4,128,256]{2,1,0:T(8,128)S(1)} %broadcast.41.clone.1, s32[128]{0:T(128)S(1)} %bitcast.32, f32[128,128,256]{2,1,0:T(8,128)} %fusion), kind=kCustom, calls=%fused_computation.5 | custom fusion | flops 4194304 | bytes 50332160 | tf_op jit(solution)/shard_map/scatter-add | solution.py:65
  748.8 0.8 add_convert_fusion
  749.5 21.8 %reduce_sum.9 = f32[256,256]{1,0:T(8,128)} reduce(f32[256,256,256]{2,1,0:T(8,128)} %bitcast.9, f32[]{:T(128)} %constant.6.clone.1), dimensions={0}, to_apply=%region_4.5 | reduce | flops 16711680 | bytes 67371008 | tf_op jit(solution)/shard_map/reduce_sum | solution.py:73
  (27 shorter events, 0.1 us)
Async XLA Ops:
  7.2 249.5 %copy-start = (bf16[512,256]{1,0:T(8,128)(2,1)S(1)}, bf16[512,256]{1,0:T(8,128)(2,1)}, u32[]{:S(2)}) copy-start(bf16[512,256]{1,0:T(8,128)(2,1)} %param.10) | copy-start | bytes 786436
  15.3 16.7 %copy-start.9 = (s32[40]{0:T(128)S(1)}, s32[40]{0:T(128)}, u32[]{:S(2)}) copy-start(s32[40]{0:T(128)} %param.13) | copy-start | bytes 484
  15.3 201.0 %copy-start.2 = (bf16[512,256]{1,0:T(8,128)(2,1)S(1)}, bf16[512,256]{1,0:T(8,128)(2,1)}, u32[]{:S(2)}) copy-start(bf16[512,256]{1,0:T(8,128)(2,1)} %param.8) | copy-start | bytes 786436
  15.3 201.0 %all-to-all-start = ((bf16[128,128,256]{2,1,0:T(8,128)(2,1)}), bf16[128,128,256]{2,1,0:T(8,128)(2,1)}, u32[]{:S(2)}, u32[]{:S(2)}) async-start(bf16[128,128,256]{2,1,0:T(8,128)(2,1)} %gather_fusion), calls=%async_computation | async-start | bytes 16777216 | tf_op jit(solution)/shard_map/all_to_all | solution.py:31
  31.3 223.5 %reduce-scatter.2.cloned.1.call-start = ((), (), s32[]{:S(2)}) async-start(), calls=%async_computation.3 | async-start | bytes 1572864 | tf_op jit(solution)/shard_map/reduce_scatter | solution.py:39
  223.9 6.0 copy-start.5
  229.9 5.0 copy-start.12
  243.9 1.0 copy-start.3
  244.9 504.6 %all-gather.3.cloned.1.call-start = ((), (), s32[]{:S(2)}) async-start(), calls=%async_computation.4 | async-start | bytes 67371008 | tf_op jit(solution)/shard_map/all_gather | solution.py:73
  255.9 0.7 copy-start.6
  257.7 10.3 %copy-start.10 = (pred[40]{0:T(512)(128)(4,1)}, pred[40]{0:T(512)(128)(4,1)S(1)}, u32[]{:S(2)}) copy-start(pred[40]{0:T(512)(128)(4,1)S(1)} %iota_compare_fusion) | copy-start | bytes 124
  261.5 6.5 copy-start.8
  268.2 3.1 copy-start.11
  271.4 2.5 copy-start.4
  305.1 405.8 %all-to-all-start.1 = ((bf16[128,128,384]{2,1,0:T(8,128)(2,1)}), bf16[128,128,384]{2,1,0:T(8,128)(2,1)}, u32[]{:S(2)}, u32[]{:S(2)}) async-start(bf16[128,128,384]{2,1,0:T(8,128)(2,1)} %copy.27), calls=%async_computation.2 | async-start | bytes 25165824 | tf_op jit(solution)/shard_map/all_to_all | solution.py:15
  319.3 5.1 copy-start.13
  324.4 9.0 %copy-start.7 = (bf16[4,128,256]{2,1,0:T(8,128)(2,1)S(1)}, bf16[4,128,256]{2,1,0:T(8,128)(2,1)}, u32[]{:S(2)}) copy-start(bf16[4,128,256]{2,1,0:T(8,128)(2,1)} %copy-done.6) | copy-start | bytes 786436
  334.4 390.3 %copy-start.14 = (s32[1,128]{1,0:T(1,128)S(1)}, s32[1,128]{1,0:T(1,128)}, u32[]{:S(2)}) copy-start(s32[1,128]{1,0:T(1,128)} %param.15) | copy-start | bytes 1540
  749.5 21.8 %copy-start.1 = (bf16[512,256]{1,0:T(8,128)(2,1)S(1)}, bf16[512,256]{1,0:T(8,128)(2,1)}, u32[]{:S(2)}) copy-start(bf16[512,256]{1,0:T(8,128)(2,1)} %param.10) | copy-start | bytes 786436
Sparse Core Ops, SparseCore 0:
  245.1 9.7 reduce-scatter.1
  259.2 463.4 all-gather.2
